TPU v7x, 512 devices: a whole 4x8x8 slice. The times are simulated.
512 devices in a mesh: seq: 64 (over z_lo, y, core), head: 8 (over z_hi, x).
Axes of the slice: x: 4, y: 8, z: 8 (z_hi: 2, z_lo: 4; z = z_hi * 4 + z_lo), core: 2. Of those that a mesh axis runs over, the one named last changes fastest.
Arguments:
- queries: bfloat16 [8192, 64, 128], P('seq', 'head'), may hold values from -11 to 11
- key_heads: bfloat16 [8192, 8, 128], P('seq', 'head'), may hold values from -20 to 20
- value_heads: bfloat16 [8192, 8, 128], P('seq', 'head'), may hold values from -6 to 6
- fold_map: int32 [64], replicated, may hold values from 0 to 63, as said below
- partner_map: int32 [2, 64], replicated, may hold values from 0 to 63, as said below
- out_weight: bfloat16 [8192, 5120], P('head', 'seq'), may hold values from -0.1875 to 0.1875
Outputs:
- projected: bfloat16 [8192, 5120], P('seq', 'head')
Inputs may be any that keep to these rules, and one draw needn't show every extreme that they name: `fold_map`: a permutation of 0 to 63. `partner_map`: round r pairs index i with index i XOR m_r, where m_r is nonzero and the two rounds have different m_r.
All inputs are finite; a program needn't handle non-finite values.
Results may differ from a plain program's by a relative error of at most 0.0051.
Values may be sent and summed in bfloat16 or wider, within the bound.
A program may use at most 64 MiB of HBM per device.

v0:
```python
import math

import jax
import jax.numpy as jnp
from jax import lax
from jax.sharding import PartitionSpec as P


def from_partner(shard, axis, distance):
    return lax.ppermute(shard, axis, [(i, i ^ 1 << distance) for i in range(lax.axis_size(axis))])


def per_device(queries, key_heads, value_heads, fold_map, partner_map, out_weight):
    my_index = lax.axis_index("seq")
    seq_count = lax.axis_size("seq")
    half_rows = queries.shape[0] // 2
    all_rows = 2 * half_rows
    local_kv = key_heads.shape[1]
    group_size = queries.shape[1] // local_kv
    head_dim = queries.shape[2]
    score_scale = 1.0 / math.sqrt(head_dim)
    query_groups = queries.reshape(all_rows, local_kv, group_size, head_dim)
    offsets = jnp.arange(half_rows, dtype=jnp.int32)

    def places_of(device):
        lower_block = fold_map[device]
        return jnp.concatenate(
            [
                lower_block * half_rows + offsets,
                (2 * seq_count - 1 - lower_block) * half_rows + offsets,
            ]
        )

    def raw_scores(query_part, key_part):
        return (
            jnp.einsum("rhje,khe->hjrk", query_part, key_part, preferred_element_type=jnp.float32)
            * score_scale
        )

    def weighted_sum(weights, value_part):
        return jnp.einsum(
            "hjrk,khe->rhje",
            weights.astype(jnp.bfloat16),
            value_part,
            preferred_element_type=jnp.float32,
        )

    my_places = places_of(my_index)
    own_scores = jnp.where(
        my_places[None, :] <= my_places[:, None], raw_scores(query_groups, key_heads), -jnp.inf
    )
    partner_a = partner_map[0, my_index]
    partner_b = partner_map[1, my_index]
    flip_a = jnp.bitwise_xor(partner_a, my_index)
    flip_b = jnp.bitwise_xor(partner_b, my_index)
    bit_count = seq_count.bit_length() - 1
    own_pair = jnp.stack([key_heads, value_heads])

    def route_pair(flip_mask):
        moving = own_pair
        for bit_index in range(bit_count):
            arrived = from_partner(moving, "seq", bit_index)
            take_this = jnp.bitwise_and(jnp.right_shift(flip_mask, bit_index), 1) == 1
            moving = jnp.where(take_this, arrived, moving)
        return moving

    pair_a = route_pair(flip_a)
    pair_b = route_pair(flip_b)
    own_max = jnp.max(own_scores, axis=-1)
    remote = []
    row_max = own_max
    for partner, moved_pair in ((partner_a, pair_a), (partner_b, pair_b)):
        their_places = places_of(partner)
        scores = jnp.where(
            their_places[None, :] <= my_places[:, None],
            raw_scores(query_groups, moved_pair[0]),
            -jnp.inf,
        )
        row_max = jnp.maximum(row_max, jnp.max(scores, axis=-1))
        remote.append((scores, moved_pair[1]))
    own_weights = jnp.exp(own_scores - row_max[..., None])
    row_total = jnp.sum(own_weights, axis=-1)
    weighted = weighted_sum(own_weights, value_heads)
    for scores, value_part in remote:
        weights = jnp.exp(scores - row_max[..., None])
        row_total = row_total + jnp.sum(weights, axis=-1)
        weighted = weighted + weighted_sum(weights, value_part)
    attended = (weighted / jnp.moveaxis(row_total, 2, 0)[..., None]).astype(jnp.bfloat16)
    flat_rows = attended.reshape(all_rows, local_kv * group_size * head_dim)
    partial_terms = jnp.dot(
        flat_rows,
        lax.all_gather(out_weight, "seq", axis=1, tiled=True),
        preferred_element_type=jnp.float32,
    )
    return lax.psum_scatter(partial_terms, "head", scatter_dimension=1, tiled=True).astype(
        jnp.bfloat16
    )


def solution(mesh):
    return jax.shard_map(
        per_device,
        mesh=mesh,
        in_specs=(
            P("seq", "head", None),
            P("seq", "head", None),
            P("seq", "head", None),
            P(),
            P(),
            P("head", "seq"),
        ),
        out_specs=P("seq", "head"),
        check_vma=False,
    )
```

profile of v0, /device:TPU:8, one launch (start us, length us, event | category | flops | bytes accessed | tf_op | source)
XLA Modules:
  0.0 270.4 jit_solution(317472850337719558)
XLA Ops:
  6.5 0.7 all-gather.2.cloned.1.call-update
  7.3 0.8 pad_maximum_fusion
  8.1 1.9 collective-permute-start
  10.0 1.4 constant_dynamic-slice_fusion.1
  15.2 1.4 fusion.31
  21.8 0.8 broadcast_select_fusion.6
  22.6 7.7 %collective-permute-start.1 = (bf16[2,128,1,128]{3,1,2,0:T(8,128)(2,1)S(1)}, bf16[2,128,1,128]{3,1,2,0:T(8,128)(2,1)S(1)}, u32[]{:S(2)}, u32[]{:S(2)}) collective-permute-start(bf16[2,128,1,128]{3,1,2,0:T(8,128)(2,1)S(1)} %get-tuple-element.8), channel_id=1, source_target_pairs={{0,16},{8,24},{16,0},{24,8},{32,48},{40,56},{48,32},{56,40},{64,80... | collective-permute-start | bytes 196616 | tf_op jit(solution)/shard_map/ppermute | solution.py:10
  30.3 1.0 fusion.33
  31.4 1.9 collective-permute-start.6
  33.3 0.3 collective-permute-done.1
  33.6 1.9 collective-permute-start.2
  35.6 3.4 %collective-permute-done.6 = bf16[2,128,1,128]{3,1,2,0:T(8,128)(2,1)S(1)} collective-permute-done((bf16[2,128,1,128]{3,1,2,0:T(8,128)(2,1)S(1)}, bf16[2,128,1,128]{3,1,2,0:T(8,128)(2,1)S(1)}, u32[]{:S(2)}, u32[]{:S(2)}) %collective-permute-start.6) | collective-permute-done | bytes 65568 | tf_op jit(solution)/shard_map/ppermute | solution.py:10
  39.0 1.9 collective-permute-start.7
  40.9 1.1 collective-permute-done.2
  42.0 1.9 collective-permute-start.3
  44.0 2.9 %collective-permute-done.7 = bf16[2,128,1,128]{3,1,2,0:T(8,128)(2,1)S(1)} collective-permute-done((bf16[2,128,1,128]{3,1,2,0:T(8,128)(2,1)S(1)}, bf16[2,128,1,128]{3,1,2,0:T(8,128)(2,1)S(1)}, u32[]{:S(2)}, u32[]{:S(2)}) %collective-permute-start.7) | collective-permute-done | bytes 65568 | tf_op jit(solution)/shard_map/ppermute | solution.py:10
  46.9 5.0 %collective-permute-start.8 = (bf16[2,128,1,128]{3,1,2,0:T(8,128)(2,1)S(1)}, bf16[2,128,1,128]{3,1,2,0:T(8,128)(2,1)S(1)}, u32[]{:S(2)}, u32[]{:S(2)}) collective-permute-start(bf16[2,128,1,128]{3,1,2,0:T(8,128)(2,1)S(1)} %broadcast_select_fusion.2), channel_id=1, source_target_pairs={{0,64},{8,72},{16,80},{24,88},{32,96},{40,104},{48,112},{56,120},{... | collective-permute-start | bytes 196616 | tf_op jit(solution)/shard_map/ppermute | solution.py:10
  51.8 1.8 collective-permute-done.3
  53.6 1.9 collective-permute-start.4
  55.5 3.6 %collective-permute-done.8 = bf16[2,128,1,128]{3,1,2,0:T(8,128)(2,1)S(1)} collective-permute-done((bf16[2,128,1,128]{3,1,2,0:T(8,128)(2,1)S(1)}, bf16[2,128,1,128]{3,1,2,0:T(8,128)(2,1)S(1)}, u32[]{:S(2)}, u32[]{:S(2)}) %collective-permute-start.8) | collective-permute-done | bytes 65568 | tf_op jit(solution)/shard_map/ppermute | solution.py:10
  59.1 1.9 collective-permute-start.9
  61.1 6.5 %collective-permute-start.5 = (bf16[2,128,1,128]{3,1,2,0:T(8,128)(2,1)S(1)}, bf16[2,128,1,128]{3,1,2,0:T(8,128)(2,1)S(1)}, u32[]{:S(2)}, u32[]{:S(2)}) collective-permute-start(bf16[2,128,1,128]{3,1,2,0:T(8,128)(2,1)S(1)} %broadcast_select_fusion.10), channel_id=1, source_target_pairs={{0,256},{8,264},{16,272},{24,280},{32,288},{40,296},{48,304},{56,3... | collective-permute-start | bytes 196616 | tf_op jit(solution)/shard_map/ppermute | solution.py:10
  67.6 2.2 collective-permute-start.10
  69.7 3.3 %collective-permute-done.5 = bf16[2,128,1,128]{3,1,2,0:T(8,128)(2,1)S(1)} collective-permute-done((bf16[2,128,1,128]{3,1,2,0:T(8,128)(2,1)S(1)}, bf16[2,128,1,128]{3,1,2,0:T(8,128)(2,1)S(1)}, u32[]{:S(2)}, u32[]{:S(2)}) %collective-permute-start.5) | collective-permute-done | bytes 65568 | tf_op jit(solution)/shard_map/ppermute | solution.py:10
  73.1 3.0 %collective-permute-done.10 = bf16[2,128,1,128]{3,1,2,0:T(8,128)(2,1)S(1)} collective-permute-done((bf16[2,128,1,128]{3,1,2,0:T(8,128)(2,1)S(1)}, bf16[2,128,1,128]{3,1,2,0:T(8,128)(2,1)S(1)}, u32[]{:S(2)}, u32[]{:S(2)}) %collective-permute-start.10) | collective-permute-done | bytes 65568 | tf_op jit(solution)/shard_map/ppermute | solution.py:10
  76.9 0.2 fusion.17
  77.2 1.0 convolution_bitcast_fusion
  78.2 0.3 fusion.9
  78.5 66.9 %all-gather.2.cloned.1.call-done = bf16[1024,5120]{0,1:T(8,128)(2,1)} async-done(((bf16[1024,80]{0,1:T(8,128)(2,1)}), bf16[1024,5120]{0,1:T(8,128)(2,1)}) %all-gather.2.cloned.1.call-update) | async-done | bytes 10485776 | tf_op jit(solution)/shard_map/all_gather | solution.py:92
  145.4 9.1 %fusion.35 = f32[128,5120]{1,0:T(8,128)} fusion(bf16[128,1024]{0,1:T(8,128)(2,1)S(1)} %bitcast.95, bf16[1024,5120]{0,1:T(8,128)(2,1)} %all-gather.2.cloned.1.call-done), kind=kOutput, calls=%fused_computation.73 | convolution fusion | flops 1342177280 | bytes 13369344 | tf_op jit(solution)/shard_map/dot_general | solution.py:90
  154.5 107.4 %reduce-scatter.2.cloned.1.call-done = f32[128,640]{1,0:T(8,128)} async-done(((f32[128,5120]{1,0:T(8,128)}), f32[128,640]{1,0:T(8,128)}) %reduce-scatter.2.cloned.1.call-update) | async-done | bytes 327696 | tf_op jit(solution)/shard_map/reduce_scatter | solution.py:95
  261.9 1.7 convert_element_type.19
  (30 shorter events, 1.3 us)
Async XLA Ops:
  6.5 23.8 %copy-start = (bf16[128,8,128]{2,1,0:T(8,128)(2,1)S(1)}, bf16[128,8,128]{2,1,0:T(8,128)(2,1)}, u32[]{:S(2)}) copy-start(bf16[128,8,128]{2,1,0:T(8,128)(2,1)} %param.6) | copy-start | bytes 786436
  6.5 138.8 %all-gather.2.cloned.1.call-start = ((), (), s32[]{:S(2)}) async-start(), calls=%async_computation.1 | async-start | bytes 10649600 | tf_op jit(solution)/shard_map/all_gather | solution.py:92
  7.3 254.7 %reduce-scatter.2.cloned.1.call-start = ((), (), s32[]{:S(2)}) async-start(), calls=%async_computation.2 | async-start | bytes 2949120 | tf_op jit(solution)/shard_map/reduce_scatter | solution.py:95
  8.1 13.7 %collective-permute-start = (bf16[2,128,1,128]{3,1,2,0:T(8,128)(2,1)S(1)}, bf16[2,128,1,128]{3,1,2,0:T(8,128)(2,1)S(1)}, u32[]{:S(2)}, u32[]{:S(2)}) collective-permute-start(bf16[2,128,1,128]{3,1,2,0:T(8,128)(2,1)S(1)} %pad_maximum_fusion), channel_id=1, source_target_pairs={{0,8},{8,0},{16,24},{24,16},{32,40},{40,32},{48,56},{56,48},{64,72... | collective-permute-start | bytes 196616 | tf_op jit(solution)/shard_map/ppermute | solution.py:10
  22.6 11.0 %collective-permute-start.1 = (bf16[2,128,1,128]{3,1,2,0:T(8,128)(2,1)S(1)}, bf16[2,128,1,128]{3,1,2,0:T(8,128)(2,1)S(1)}, u32[]{:S(2)}, u32[]{:S(2)}) collective-permute-start(bf16[2,128,1,128]{3,1,2,0:T(8,128)(2,1)S(1)} %get-tuple-element.8), channel_id=1, source_target_pairs={{0,16},{8,24},{16,0},{24,8},{32,48},{40,56},{48,32},{56,40},{64,80... | collective-permute-start | bytes 196616 | tf_op jit(solution)/shard_map/ppermute | solution.py:10
  31.4 7.6 %collective-permute-start.6 = (bf16[2,128,1,128]{3,1,2,0:T(8,128)(2,1)S(1)}, bf16[2,128,1,128]{3,1,2,0:T(8,128)(2,1)S(1)}, u32[]{:S(2)}, u32[]{:S(2)}) collective-permute-start(bf16[2,128,1,128]{3,1,2,0:T(8,128)(2,1)S(1)} %get-tuple-element.9), channel_id=1, source_target_pairs={{0,16},{8,24},{16,0},{24,8},{32,48},{40,56},{48,32},{56,40},{64,80... | collective-permute-start | bytes 196616 | tf_op jit(solution)/shard_map/ppermute | solution.py:10
  33.6 8.4 %collective-permute-start.2 = (bf16[2,128,1,128]{3,1,2,0:T(8,128)(2,1)S(1)}, bf16[2,128,1,128]{3,1,2,0:T(8,128)(2,1)S(1)}, u32[]{:S(2)}, u32[]{:S(2)}) collective-permute-start(bf16[2,128,1,128]{3,1,2,0:T(8,128)(2,1)S(1)} %broadcast_select_fusion.7), channel_id=1, source_target_pairs={{0,32},{8,40},{16,48},{24,56},{32,0},{40,8},{48,16},{56,24},{64,96... | collective-permute-start | bytes 196616 | tf_op jit(solution)/shard_map/ppermute | solution.py:10
  39.0 7.8 %collective-permute-start.7 = (bf16[2,128,1,128]{3,1,2,0:T(8,128)(2,1)S(1)}, bf16[2,128,1,128]{3,1,2,0:T(8,128)(2,1)S(1)}, u32[]{:S(2)}, u32[]{:S(2)}) collective-permute-start(bf16[2,128,1,128]{3,1,2,0:T(8,128)(2,1)S(1)} %broadcast_select_fusion.1), channel_id=1, source_target_pairs={{0,32},{8,40},{16,48},{24,56},{32,0},{40,8},{48,16},{56,24},{64,96... | collective-permute-start | bytes 196616 | tf_op jit(solution)/shard_map/ppermute | solution.py:10
  42.0 11.6 %collective-permute-start.3 = (bf16[2,128,1,128]{3,1,2,0:T(8,128)(2,1)S(1)}, bf16[2,128,1,128]{3,1,2,0:T(8,128)(2,1)S(1)}, u32[]{:S(2)}, u32[]{:S(2)}) collective-permute-start(bf16[2,128,1,128]{3,1,2,0:T(8,128)(2,1)S(1)} %broadcast_select_fusion.8), channel_id=1, source_target_pairs={{0,64},{8,72},{16,80},{24,88},{32,96},{40,104},{48,112},{56,120},{... | collective-permute-start | bytes 196616 | tf_op jit(solution)/shard_map/ppermute | solution.py:10
  46.9 12.2 %collective-permute-start.8 = (bf16[2,128,1,128]{3,1,2,0:T(8,128)(2,1)S(1)}, bf16[2,128,1,128]{3,1,2,0:T(8,128)(2,1)S(1)}, u32[]{:S(2)}, u32[]{:S(2)}) collective-permute-start(bf16[2,128,1,128]{3,1,2,0:T(8,128)(2,1)S(1)} %broadcast_select_fusion.2), channel_id=1, source_target_pairs={{0,64},{8,72},{16,80},{24,88},{32,96},{40,104},{48,112},{56,120},{... | collective-permute-start | bytes 196616 | tf_op jit(solution)/shard_map/ppermute | solution.py:10
  53.6 7.4 %collective-permute-start.4 = (bf16[2,128,1,128]{3,1,2,0:T(8,128)(2,1)S(1)}, bf16[2,128,1,128]{3,1,2,0:T(8,128)(2,1)S(1)}, u32[]{:S(2)}, u32[]{:S(2)}) collective-permute-start(bf16[2,128,1,128]{3,1,2,0:T(8,128)(2,1)S(1)} %broadcast_select_fusion.9), channel_id=1, source_target_pairs={{0,128},{8,136},{16,144},{24,152},{32,160},{40,168},{48,176},{56,1... | collective-permute-start | bytes 196616 | tf_op jit(solution)/shard_map/ppermute | solution.py:10
  59.1 8.4 %collective-permute-start.9 = (bf16[2,128,1,128]{3,1,2,0:T(8,128)(2,1)S(1)}, bf16[2,128,1,128]{3,1,2,0:T(8,128)(2,1)S(1)}, u32[]{:S(2)}, u32[]{:S(2)}) collective-permute-start(bf16[2,128,1,128]{3,1,2,0:T(8,128)(2,1)S(1)} %broadcast_select_fusion.3), channel_id=1, source_target_pairs={{0,128},{8,136},{16,144},{24,152},{32,160},{40,168},{48,176},{56,1... | collective-permute-start | bytes 196616 | tf_op jit(solution)/shard_map/ppermute | solution.py:10
  61.1 12.0 %collective-permute-start.5 = (bf16[2,128,1,128]{3,1,2,0:T(8,128)(2,1)S(1)}, bf16[2,128,1,128]{3,1,2,0:T(8,128)(2,1)S(1)}, u32[]{:S(2)}, u32[]{:S(2)}) collective-permute-start(bf16[2,128,1,128]{3,1,2,0:T(8,128)(2,1)S(1)} %broadcast_select_fusion.10), channel_id=1, source_target_pairs={{0,256},{8,264},{16,272},{24,280},{32,288},{40,296},{48,304},{56,3... | collective-permute-start | bytes 196616 | tf_op jit(solution)/shard_map/ppermute | solution.py:10
  67.6 8.6 %collective-permute-start.10 = (bf16[2,128,1,128]{3,1,2,0:T(8,128)(2,1)S(1)}, bf16[2,128,1,128]{3,1,2,0:T(8,128)(2,1)S(1)}, u32[]{:S(2)}, u32[]{:S(2)}) collective-permute-start(bf16[2,128,1,128]{3,1,2,0:T(8,128)(2,1)S(1)} %broadcast_select_fusion.4), channel_id=1, source_target_pairs={{0,256},{8,264},{16,272},{24,280},{32,288},{40,296},{48,304},{56,3... | collective-permute-start | bytes 196616 | tf_op jit(solution)/shard_map/ppermute | solution.py:10
Sparse Core Ops, SparseCore 0:
  9.5 135.8 all-gather.1
  154.7 107.2 reduce-scatter.1
where the time goes:
time: 271 us; the launch traced here: 270 us
  waiting for transfers between devices  194 us (72%)
  starting transfers between devices  34.8 us (13%)
  between operations  22.3 us (8%)
  matrix products  12.2 us (5%)
  other arithmetic  3.94 us (1%)
  local copies, waits for them, and re-layouts  2.74 us (1%)
    reduce_scatter x1, waiting for transfers between devices, per_device(): lax.psum_scatter(partial_terms, 'head', scatter_dimension=1, tiled=True)  107 us
    all_gather x1, waiting for transfers between devices, per_device(): lax.all_gather(out_weight, 'seq', axis=1, tiled=True)  66.9 us
    ppermute x11, starting transfers between devices, from_partner(): lax.ppermute(shard, axis, [(i, i ^ 1 << distance) for i in range(lax.axis...  34.8 us
    ppermute x11, waiting for transfers between devices, from_partner(): lax.ppermute(shard, axis, [(i, i ^ 1 << distance) for i in range(lax.axis...  19.4 us
    dot_general x1, matrix products, per_device(): jnp.dot(flat_rows, lax.all_gather(out_weight, 'seq', axis=1, tiled=True),...  9.14 us
  transfers between devices with their start and end apart: 13, of which 10 were waited for; matrix products, arithmetic and copies ran while one was open for 3% of the time, Pallas kernels for 0%

commit v1 on v0

v1 whole, which is shorter than its diff:
```python
import math

import jax
import jax.numpy as jnp
from jax import lax
from jax.experimental import pallas as pl
from jax.experimental.pallas import tpu as pltpu
from jax.sharding import PartitionSpec as P

MESH = pl.DeviceIdType.MESH
HEADS = 8
DIM = 128
ROWS = 128
HALF = 64
DEPTH = HEADS * DIM
CHUNK = 80
QUARTER = 320
N_Y = 8
BLOCKS = 128


def dot_nt(a, b):
    return lax.dot_general(a, b, (((1,), (1,)), ((), ())), preferred_element_type=jnp.float32)


def dot_nn(a, b):
    return lax.dot_general(a, b, (((1,), (0,)), ((), ())), preferred_element_type=jnp.float32)


def kernel(
    q_ref, k_ref, v_ref, fold_ref, partner_ref, w_ref, out_ref,
    kv_y, kv_z1, kv_z2, kv_c, q_wide, q_heads, k_all, v_all,
    w_all, att, x1_out, x1_in, x2_out, x2_in, kept, s2_out, s2_in,
    kv_send, kv_recv, w_send, w_recv, pair_send, pair_recv,
    step_send, step_recv, att_send, att_recv, x_send, x_recv, s2_send, s2_recv,
):
    seq = lax.axis_index("seq")
    head = lax.axis_index("head")
    z, y, core = seq // 16, (seq // 2) % 8, seq % 2
    z_hi, x = head // 4, head % 4

    def at(z_to, y_to, core_to):
        return z_to * 16 + y_to * 2 + core_to

    up = (at(z, (y + 1) % 8, core), head)
    down = (at(z, (y + 7) % 8, core), head)
    z_flip = [None, (seq ^ 16, head), (seq ^ 32, head)]
    other_core = (seq ^ 1, head)
    x_flip = {1: (seq, head ^ 1), 3: (seq, head ^ 3)}

    target_head = 2 * z + x // 2
    targets = [(seq ^ (16 * t), target_head) for t in range(4)]
    home = target_head == head
    source_seq = at(head // 2, y, core)

    barrier = pltpu.get_barrier_semaphore()
    for peer in (up, down, z_flip[1], z_flip[2], other_core, x_flip[1], x_flip[3]):
        pl.semaphore_signal(barrier, inc=1, device_id=peer, device_id_type=MESH)
    for hi in range(2):
        for side in range(2):
            source_head = hi * 4 + 2 * (head % 2) + side
            mine = jnp.logical_and(source_seq == seq, source_head == head)

            @pl.when(jnp.logical_not(mine))
            def _():
                pl.semaphore_signal(
                    barrier, inc=1, device_id=(source_seq, source_head), device_id_type=MESH
                )

    kv_y[0, 0:ROWS, :] = k_ref[...]
    kv_y[0, ROWS:, :] = jnp.transpose(v_ref[...].astype(jnp.float32)).astype(jnp.bfloat16)
    pl.semaphore_wait(barrier, 11 - jnp.where(home, 1, 0))

    def remote(src, dst, send, recv, peer):
        copy = pltpu.make_async_remote_copy(
            src_ref=src, dst_ref=dst, send_sem=send, recv_sem=recv,
            device_id=peer, device_id_type=MESH,
        )
        copy.start()
        return copy

    sent = []

    def kv_step(way, k):
        src_slot = k - 1 if way == 0 else (8 - (k - 1)) % 8
        dst_slot = k if way == 0 else 8 - k
        src, dst = kv_y.at[src_slot], kv_y.at[dst_slot]
        if k == 4:
            part = pl.ds(ROWS * way, ROWS)
            src, dst = kv_y.at[src_slot, part], kv_y.at[dst_slot, part]
        copy = remote(
            src, dst, kv_send.at[way, k - 1], kv_recv.at[way, k - 1], up if way == 0 else down
        )
        sent.append(copy)
        return copy

    def w_rows(k):
        return pl.multiple_of((((y - k) % 8) * 2 + core) * CHUNK, 16)

    def w_step(way, k):
        slot = k - 1 if way == 0 else (8 - (k - 1)) % 8
        first = w_rows(slot)
        rows = CHUNK
        if k == 4:
            first, rows = (first, 48) if way == 0 else (first + 48, 32)
        place = pl.ds(pl.multiple_of(first, 16), rows)
        copy = remote(
            w_all.at[place], w_all.at[place], w_send.at[way, k - 1], w_recv.at[way, k - 1],
            up if way == 0 else down,
        )
        sent.append(copy)
        return copy

    def w_pair(k):
        place = pl.ds(w_rows(k), CHUNK)
        copy = remote(
            w_all.at[place], w_all.at[place], pair_send.at[k], pair_recv.at[k], other_core
        )
        sent.append(copy)
        return copy

    kv_up, kv_down = kv_step(0, 1), kv_step(1, 1)
    w_all[pl.ds(w_rows(0), CHUNK), :] = w_ref[...]
    pairs = [w_pair(0)]
    q_wide[...] = q_ref[...].astype(jnp.float32)
    for k in range(2, 5):
        kv_up.wait_recv()
        kv_up = kv_step(0, k)
        kv_down.wait_recv()
        kv_down = kv_step(1, k)
        if k == 2:
            for h in range(HEADS):
                q_heads[pl.ds(h * ROWS, ROWS), :] = q_wide[
                    pl.ds(h, ROWS, stride=HEADS), :
                ].astype(jnp.bfloat16)
    w_up, w_down = w_step(0, 1), w_step(1, 1)
    k_all[0:ROWS, :] = k_ref[...]
    v_all[:, 0:ROWS] = kv_y[0, ROWS:, :]
    kv_up.wait_recv()
    kv_down.wait_recv()

    partners = [partner_ref[0, seq], partner_ref[1, seq]]
    flips = [partner ^ seq for partner in partners]

    for i in range(2):
        y_from = (partners[i] >> 1) & 7
        kv_z1[0, i] = kv_y[(y - y_from) & 7]
    step = remote(kv_z1.at[0], kv_z1.at[1], step_send.at[0], step_recv.at[0], z_flip[1])
    sent.append(step)

    step.wait_recv()
    for i in range(2):
        kv_z2[0, i] = kv_z1[(flips[i] >> 4) & 1, i]
    step = remote(kv_z2.at[0], kv_z2.at[1], step_send.at[1], step_recv.at[1], z_flip[2])
    sent.append(step)

    w_up.wait_recv()
    w_up = w_step(0, 2)
    w_down.wait_recv()
    w_down = w_step(1, 2)
    pairs += [w_pair(1), w_pair(7)]

    step.wait_recv()
    for i in range(2):
        kv_c[0, i] = kv_z2[(flips[i] >> 5) & 1, i]
    step = remote(kv_c.at[0], kv_c.at[1], step_send.at[2], step_recv.at[2], other_core)
    sent.append(step)

    w_up.wait_recv()
    w_up = w_step(0, 3)
    w_down.wait_recv()
    w_down = w_step(1, 3)
    pairs += [w_pair(2), w_pair(6)]

    step.wait_recv()
    for i in range(2):
        from_core = flips[i] & 1
        k_all[pl.ds((i + 1) * ROWS, ROWS), :] = kv_c[from_core, i, 0:ROWS, :]
        v_all[:, pl.ds((i + 1) * ROWS, ROWS)] = kv_c[from_core, i, ROWS:, :]

    def places(fold, offset):
        return offset + jnp.where(
            offset < HALF, fold * HALF, (BLOCKS - 1 - fold) * HALF - HALF
        )

    down_iota = lax.broadcasted_iota(jnp.int32, (ROWS, ROWS), 0)
    across_iota = lax.broadcasted_iota(jnp.int32, (ROWS, ROWS), 1)
    own_places = places(fold_ref[seq], across_iota)
    hidden = []
    for device in (seq, partners[0], partners[1]):
        seen = places(fold_ref[device], down_iota) <= own_places
        hidden.append(jnp.where(seen, 0.0, -jnp.inf).astype(jnp.float32))
    bias = jnp.concatenate(hidden, axis=0)
    bias = jnp.concatenate([bias] * 4, axis=1)
    scale = 1.0 / math.sqrt(DIM)
    att_copies = {}

    for part in range(2):
        heads = pl.ds(part * 4 * ROWS, 4 * ROWS)
        scores = dot_nt(k_all[...], q_heads[heads, :]) * scale + bias
        top = jnp.max(scores, axis=0, keepdims=True)
        weights = jnp.exp(scores - top)
        total = jnp.sum(weights, axis=0, keepdims=True)
        summed = dot_nn(v_all[...], weights.astype(jnp.bfloat16)) / total
        summed = summed.astype(jnp.bfloat16)
        for h in range(4):
            att[0, pl.ds((part * 4 + h) * DIM, DIM), :] = summed[:, h * ROWS : (h + 1) * ROWS]
        span = pl.ds(part * DEPTH // 2, DEPTH // 2)
        for t in (1, 2):
            copy = remote(
                att.at[0, span], att.at[t, span],
                att_send.at[t - 1, part], att_recv.at[t - 1, part], z_flip[t],
            )
            sent.append(copy)
            att_copies[t, part] = copy

    w_up.wait_recv()
    w_up = w_step(0, 4)
    w_down.wait_recv()
    w_down = w_step(1, 4)
    pairs += [w_pair(3), w_pair(5)]
    w_up.wait_recv()
    w_down.wait_recv()
    pairs.append(w_pair(4))
    for copy in pairs:
        copy.wait_recv()

    x1_copies, x2_copies = [], []

    def ways(t):
        return (1, 3) if t % 2 == 0 else (3, 1)

    def product(t, quarter):
        rows = pl.ds(pl.multiple_of(quarter * QUARTER, 16), QUARTER)
        return dot_nn(w_all[rows, :], att[t])

    def project(t):
        first, second = ways(t)
        x1_out[t, 0] = product(t, x ^ first).astype(jnp.bfloat16)
        x1_out[t, 1] = product(t, x ^ 2).astype(jnp.bfloat16)
        copy = remote(x1_out.at[t], x1_in.at[t], x_send.at[0, t], x_recv.at[0, t], x_flip[first])
        sent.append(copy)
        x1_copies.append(copy)
        kept[t, 1] = product(t, x ^ second)
        kept[t, 0] = product(t, x)

    def second_sum(t):
        second = ways(t)[1]
        x1_copies[t].wait_recv()
        x2_out[t] = (kept[t, 1] + x1_in[t, 1].astype(jnp.float32)).astype(jnp.bfloat16)
        copy = remote(x2_out.at[t], x2_in.at[t], x_send.at[1, t], x_recv.at[1, t], x_flip[second])
        sent.append(copy)
        x2_copies.append(copy)
        kept[t, 0] = kept[t, 0] + x1_in[t, 0].astype(jnp.float32)

    slot_side = x % 2

    def deliver(t):
        x2_copies[t].wait_recv()
        s2_out[t] = (kept[t, 0] + x2_in[t].astype(jnp.float32)).astype(jnp.bfloat16)

        def away():
            pltpu.make_async_remote_copy(
                src_ref=s2_out.at[t], dst_ref=s2_in.at[z_hi, slot_side],
                send_sem=s2_send.at[t], recv_sem=s2_recv.at[z_hi, slot_side],
                device_id=targets[t], device_id_type=MESH,
            ).start()

        if t:
            away()
        else:
            pl.when(jnp.logical_not(home))(away)

            @pl.when(home)
            def _():
                pltpu.make_async_copy(
                    s2_out.at[t], s2_in.at[z_hi, slot_side], s2_recv.at[z_hi, slot_side]
                ).start()

    def wait_att(t):
        for part in range(2):
            att_copies[t, part].wait_recv()

    project(0)
    wait_att(1)
    project(1)
    second_sum(0)
    for part in range(2):
        att_copies[2, part].wait_recv()
        span = pl.ds(part * DEPTH // 2, DEPTH // 2)
        copy = remote(
            att.at[2, span], att.at[3, span], att_send.at[2, part], att_recv.at[2, part],
            z_flip[1],
        )
        sent.append(copy)
        att_copies[3, part] = copy
    project(2)
    second_sum(1)
    deliver(0)
    second_sum(2)
    deliver(1)
    wait_att(3)
    project(3)
    deliver(2)
    second_sum(3)
    deliver(3)

    def last(t, hi, side):
        return pltpu.make_async_remote_copy(
            src_ref=s2_out.at[t], dst_ref=s2_in.at[hi, side],
            send_sem=s2_send.at[t], recv_sem=s2_recv.at[hi, side],
            device_id=targets[t], device_id_type=MESH,
        )

    for side in range(2):
        for hi in range(2):
            last(1, hi, side).wait_recv()
    both = s2_in[0].astype(jnp.float32) + s2_in[1].astype(jnp.float32)
    both = both.reshape(2 * QUARTER, ROWS)
    out_ref[...] = jnp.transpose(both).astype(jnp.bfloat16)

    for copy in sent:
        copy.wait_send()
    for t in range(1, 4):
        last(t, 0, 0).wait_send()

    @pl.when(jnp.logical_not(home))
    def _():
        last(0, 0, 0).wait_send()


def per_device(queries, key_heads, value_heads, fold_map, partner_map, out_weight):
    vmem = pl.BlockSpec(memory_space=pltpu.VMEM)
    smem = pl.BlockSpec(memory_space=pltpu.SMEM)
    bf16, f32 = jnp.bfloat16, jnp.float32
    dma = pltpu.SemaphoreType.DMA
    kv_rows = 2 * ROWS
    return pl.pallas_call(
        kernel,
        out_shape=jax.ShapeDtypeStruct((ROWS, 2 * QUARTER), bf16),
        in_specs=[vmem, vmem, vmem, smem, smem, vmem],
        out_specs=vmem,
        scratch_shapes=[
            pltpu.VMEM((N_Y, kv_rows, DIM), bf16),
            pltpu.VMEM((2, 2, kv_rows, DIM), bf16),
            pltpu.VMEM((2, 2, kv_rows, DIM), bf16),
            pltpu.VMEM((2, 2, kv_rows, DIM), bf16),
            pltpu.VMEM((DEPTH, DIM), f32),
            pltpu.VMEM((DEPTH, DIM), bf16),
            pltpu.VMEM((3 * ROWS, DIM), bf16),
            pltpu.VMEM((DIM, 3 * ROWS), bf16),
            pltpu.VMEM((16 * CHUNK, DEPTH), bf16),
            pltpu.VMEM((4, DEPTH, ROWS), bf16),
            pltpu.VMEM((4, 2, QUARTER, ROWS), bf16),
            pltpu.VMEM((4, 2, QUARTER, ROWS), bf16),
            pltpu.VMEM((4, QUARTER, ROWS), bf16),
            pltpu.VMEM((4, QUARTER, ROWS), bf16),
            pltpu.VMEM((4, 2, QUARTER, ROWS), f32),
            pltpu.VMEM((4, QUARTER, ROWS), bf16),
            pltpu.VMEM((2, 2, QUARTER, ROWS), bf16),
            dma((2, 4)), dma((2, 4)), dma((2, 4)), dma((2, 4)), dma((8,)), dma((8,)),
            dma((3,)), dma((3,)), dma((3, 2)), dma((3, 2)), dma((2, 4)), dma((2, 4)),
            dma((4,)), dma((2, 2)),
        ],
        compiler_params=pltpu.CompilerParams(
            collective_id=0, has_side_effects=True, vmem_limit_bytes=40 * 1024 * 1024
        ),
        cost_estimate=pl.CostEstimate(
            flops=1_550_000_000, bytes_accessed=1_000_000, transcendentals=400_000
        ),
    )(
        queries.reshape(ROWS * HEADS, DIM),
        key_heads.reshape(ROWS, DIM),
        value_heads.reshape(ROWS, DIM),
        fold_map,
        partner_map,
        out_weight.T,
    )


def solution(mesh):
    return jax.shard_map(
        per_device,
        mesh=mesh,
        in_specs=(
            P("seq", "head", None),
            P("seq", "head", None),
            P("seq", "head", None),
            P(),
            P(),
            P("head", "seq"),
        ),
        out_specs=P("seq", "head"),
        check_vma=False,
    )
```

time: 271 us -> 86.8 us (0.32)
  the two profiles are of different devices: /device:TPU:8 before, /device:TPU:132 now
where the time goes in v1:
time: 86.8 us; the launch traced here: 86.5 us
  Pallas kernels  81.7 us (94%)
  local copies, waits for them, and re-layouts  4.73 us (5%)
    pallas_call x1, Pallas kernels, per_device(): pl.pallas_call(kernel, out_shape=jax.ShapeDtypeStruct((ROWS, 2 * QUARTER)...  81.7 us
    unnamed x13, local copies, waits for them, and re-layouts  4.73 us

profile of v1, /device:TPU:132, one launch (start us, length us, event | category | flops | bytes accessed | tf_op | source)
XLA Modules:
  0.0 86.5 jit_solution(1078226520352833165)
XLA Ops:
  0.0 0.0 copy-start.4
  0.0 0.0 copy-start.5
  0.0 0.7 copy-done.4
  0.7 0.0 copy-done.5
  0.7 0.0 copy-start
  0.7 0.9 %copy-done = bf16[128,8,128]{2,1,0:T(8,128)(2,1)S(1)} copy-done((bf16[128,8,128]{2,1,0:T(8,128)(2,1)S(1)}, bf16[128,8,128]{2,1,0:T(8,128)(2,1)}, u32[]{:S(2)}) %copy-start) | copy-done | bytes 262168
  1.6 0.0 copy-start.1
  1.6 0.9 %copy-done.1 = bf16[1024,80]{0,1:T(8,128)(2,1)S(1)} copy-done((bf16[1024,80]{0,1:T(8,128)(2,1)S(1)}, bf16[1024,80]{0,1:T(8,128)(2,1)}, u32[]{:S(2)}) %copy-start.1) | copy-done | bytes 163864
  2.5 0.0 copy-start.2
  2.6 0.8 copy-done.2
  3.3 0.0 copy-start.3
  3.3 0.8 copy-done.3
  4.1 81.7 %shard_map.64 = bf16[128,640]{1,0:T(8,128)(2,1)S(1)} custom-call(bf16[1024,128]{1,0:T(8,128)(2,1)S(1)} %bitcast.4, bf16[128,128]{1,0:T(8,128)(2,1)S(1)} %bitcast.6, bf16[128,128]{1,0:T(8,128)(2,1)S(1)} %bitcast.7, s32[64]{0:T(128)S(1)} %copy-done.5, s32[2,64]{1,0:T(2,128)S(1)} %copy-done.4, bf16[80,1024]{1,0:T(8,128)(2,1)S(1)} %bitcast.5), custom_call_target="tpu_custom_call" | custom-call | flops 1550000000 | bytes 1000000 | tf_op jit(solution)/shard_map/pallas_call | solution.py:338
  85.8 0.7 copy.8
Async XLA Ops:
  0.0 0.7 copy-start.4
  0.0 0.7 copy-start.5
  0.7 1.0 %copy-start = (bf16[128,8,128]{2,1,0:T(8,128)(2,1)S(1)}, bf16[128,8,128]{2,1,0:T(8,128)(2,1)}, u32[]{:S(2)}) copy-start(bf16[128,8,128]{2,1,0:T(8,128)(2,1)} %param.6) | copy-start | bytes 786436
  1.6 0.9 %copy-start.1 = (bf16[1024,80]{0,1:T(8,128)(2,1)S(1)}, bf16[1024,80]{0,1:T(8,128)(2,1)}, u32[]{:S(2)}) copy-start(bf16[1024,80]{0,1:T(8,128)(2,1)} %param.11) | copy-start | bytes 491524
  2.5 0.8 copy-start.2
  3.3 0.8 copy-start.3

commit v2 on v1

v2 whole, which is shorter than its diff:
```python
import math

import jax
import jax.numpy as jnp
from jax import lax
from jax.experimental import pallas as pl
from jax.experimental.pallas import tpu as pltpu
from jax.sharding import PartitionSpec as P

MESH = pl.DeviceIdType.MESH
HEADS = 8
DIM = 128
ROWS = 128
HALF = 64
DEPTH = HEADS * DIM
CHUNK = 80
QUARTER = 320
N_Y = 8
BLOCKS = 128


def dot_nt(a, b):
    return lax.dot_general(a, b, (((1,), (1,)), ((), ())), preferred_element_type=jnp.float32)


def dot_nn(a, b):
    return lax.dot_general(a, b, (((1,), (0,)), ((), ())), preferred_element_type=jnp.float32)


def kernel(
    q_hbm, k_hbm, v_hbm, fold_ref, partner_ref, w_hbm, out_ref,
    q_in, k_in, v_in, q_wide, q_all, kv_own, kv_y, kv_c, kv_z, w_all, att,
    kept, x_out, x_in, s2_out, s2_in,
    in_sem, y_send, y_recv, w_send, w_recv, pair_send, pair_recv, core_send, core_recv,
    q_send, q_recv, own_send, own_recv, z_send, z_recv, x_send, x_recv, s2_send, s2_recv,
):
    seq = lax.axis_index("seq")
    head = lax.axis_index("head")
    z, y, core = seq // 16, (seq // 2) % 8, seq % 2
    z_hi, x = head // 4, head % 4

    def at(z_to, y_to, core_to):
        return z_to * 16 + y_to * 2 + core_to

    def w_rows(k):
        return pl.multiple_of((((y - k) % 8) * 2 + core) * CHUNK, 16)

    w_own = pl.ds(w_rows(0), CHUNK)
    loads = [
        pltpu.make_async_copy(src, dst, in_sem.at[i])
        for i, (src, dst) in enumerate(
            ((k_hbm, k_in), (v_hbm, v_in), (q_hbm, q_in), (w_hbm, w_all.at[w_own]))
        )
    ]
    for load in loads:
        load.start()

    y_peer = {k: (at(z, (y + k) % 8, core), head) for k in (1, 2, 6, 7)}
    z_peer = {t: (seq ^ (16 * t), head) for t in (1, 2, 3)}
    x_peer = {d: (seq, head ^ d) for d in (1, 2, 3)}
    other_core = (seq ^ 1, head)

    target_head = 2 * z + x // 2
    targets = [(seq ^ (16 * t), target_head) for t in range(4)]
    home = target_head == head
    source_seq = at(head // 2, y, core)

    barrier = pltpu.get_barrier_semaphore()
    peers = [*y_peer.values(), *z_peer.values(), *x_peer.values(), other_core]
    for peer in peers:
        pl.semaphore_signal(barrier, inc=1, device_id=peer, device_id_type=MESH)
    for hi in range(2):
        for side in range(2):
            source_head = hi * 4 + 2 * (head % 2) + side
            mine = jnp.logical_and(source_seq == seq, source_head == head)

            @pl.when(jnp.logical_not(mine))
            def _():
                pl.semaphore_signal(
                    barrier, inc=1, device_id=(source_seq, source_head), device_id_type=MESH
                )

    loads[0].wait()
    loads[1].wait()
    kv_y[0, 0:ROWS, :] = k_in[...]
    kv_y[0, ROWS:, :] = jnp.transpose(v_in[...].astype(jnp.float32)).astype(jnp.bfloat16)
    loads[2].wait()
    q_wide[...] = q_in[...].astype(jnp.float32)
    for h in range(HEADS):
        q_all[0, pl.ds(h * ROWS, ROWS), :] = q_wide[
            pl.ds(h, ROWS, stride=HEADS), :
        ].astype(jnp.bfloat16)
    loads[3].wait()
    pl.semaphore_wait(barrier, len(peers) + 4 - jnp.where(home, 1, 0))

    sent = []

    def remote(src, dst, send, recv, peer):
        copy = pltpu.make_async_remote_copy(
            src_ref=src, dst_ref=dst, send_sem=send, recv_sem=recv,
            device_id=peer, device_id_type=MESH,
        )
        copy.start()
        sent.append(copy)
        return copy

    def kv_near(k):
        return remote(kv_y.at[0], kv_y.at[k], y_send.at[k], y_recv.at[k], y_peer[k])

    def kv_far(i, from_slot, to_slot, peer, part):
        return remote(
            kv_y.at[from_slot, part], kv_y.at[to_slot, part],
            y_send.at[i], y_recv.at[i], y_peer[peer],
        )

    def w_near(k):
        return remote(w_all.at[w_own], w_all.at[w_own], w_send.at[k], w_recv.at[k], y_peer[k])

    def w_far(i, slot, peer, first, rows):
        place = pl.ds(pl.multiple_of(w_rows(slot) + first, 16), rows)
        return remote(w_all.at[place], w_all.at[place], w_send.at[i], w_recv.at[i], y_peer[peer])

    def w_pair(k):
        place = pl.ds(w_rows(k), CHUNK)
        return remote(w_all.at[place], w_all.at[place], pair_send.at[k], pair_recv.at[k], other_core)

    kv_a = {k: kv_near(k) for k in (1, 7, 2, 6)}
    q_copy = {
        t: remote(q_all.at[0], q_all.at[t], q_send.at[t], q_recv.at[t], z_peer[t]) for t in (1, 2)
    }
    own_copy = {
        t: remote(kv_y.at[0], kv_own.at[t], own_send.at[t], own_recv.at[t], z_peer[t])
        for t in (1, 2)
    }
    kv_own[0] = kv_y[0]
    pairs = [w_pair(0)]

    lower, upper, whole = pl.ds(0, ROWS), pl.ds(ROWS, ROWS), pl.ds(0, 2 * ROWS)
    kv_a[2].wait_recv()
    kv_b = [kv_far(3, 2, 3, 1, whole), kv_far(4, 2, 4, 2, lower)]
    kv_a[6].wait_recv()
    kv_b += [kv_far(5, 6, 5, 7, whole), kv_far(0, 6, 4, 6, upper)]
    w_a = {k: w_near(k) for k in (1, 7, 2, 6)}
    kv_a[1].wait_recv()
    kv_a[7].wait_recv()
    for copy in kv_b:
        copy.wait_recv()

    partners = [partner_ref[0, seq], partner_ref[1, seq]]
    flips = [partner ^ seq for partner in partners]
    for i in range(2):
        kv_c[0, i] = kv_y[(y - (partners[i] >> 1)) & 7]
    step = remote(kv_c.at[0], kv_c.at[1], core_send.at[0], core_recv.at[0], other_core)
    step.wait_recv()
    for i in range(2):
        kv_z[0, i] = kv_c[flips[i] & 1, i]
    kv_step = [
        remote(kv_z.at[0], kv_z.at[t], z_send.at[t], z_recv.at[t], z_peer[t]) for t in (1, 2, 3)
    ]
    own_copy[2].wait_recv()
    own_copy[3] = remote(kv_own.at[2], kv_own.at[3], own_send.at[3], own_recv.at[3], z_peer[1])
    q_copy[2].wait_recv()
    q_copy[3] = remote(q_all.at[2], q_all.at[3], q_send.at[3], q_recv.at[3], z_peer[1])

    w_a[2].wait_recv()
    w_b = [w_far(3, 2, 1, 0, CHUNK), w_far(4, 2, 2, 0, 48)]
    w_a[6].wait_recv()
    w_b += [w_far(5, 6, 7, 0, CHUNK), w_far(0, 6, 6, 48, 32)]
    pairs += [w_pair(2), w_pair(6)]
    w_a[1].wait_recv()
    w_a[7].wait_recv()
    pairs += [w_pair(1), w_pair(7)]

    for copy in kv_step:
        copy.wait_recv()

    def places(fold, offset):
        return offset + jnp.where(
            offset < HALF, fold * HALF, (BLOCKS - 1 - fold) * HALF - HALF
        )

    down_iota = lax.broadcasted_iota(jnp.int32, (ROWS, ROWS), 0)
    across_iota = lax.broadcasted_iota(jnp.int32, (ROWS, ROWS), 1)
    scale = 1.0 / math.sqrt(DIM)

    def attend(t):
        if t % 2:
            q_copy[t].wait_recv()
            own_copy[t].wait_recv()
        device = seq ^ (16 * t)
        own_places = places(fold_ref[device], across_iota)
        hidden = []
        for source in (device, partner_ref[0, device], partner_ref[1, device]):
            seen = places(fold_ref[source], down_iota) <= own_places
            hidden.append(jnp.where(seen, 0.0, -jnp.inf).astype(jnp.float32))
        bias = jnp.concatenate(hidden, axis=0)
        bias = jnp.concatenate([bias] * 4, axis=1)
        blocks = [kv_own[t]]
        for i in range(2):
            blocks.append(kv_z[t ^ ((flips[i] >> 4) & 3), i])
        keys = jnp.concatenate([block[0:ROWS, :] for block in blocks], axis=0)
        values = jnp.concatenate([block[ROWS:, :] for block in blocks], axis=1)
        for part in range(2):
            scores = dot_nt(keys, q_all[t, pl.ds(part * 4 * ROWS, 4 * ROWS), :]) * scale + bias
            top = jnp.max(scores, axis=0, keepdims=True)
            weights = jnp.exp(scores - top)
            total = jnp.sum(weights, axis=0, keepdims=True)
            summed = dot_nn(values, weights.astype(jnp.bfloat16)) / total
            summed = summed.astype(jnp.bfloat16)
            for h in range(4):
                att[t, pl.ds((part * 4 + h) * DIM, DIM), :] = summed[:, h * ROWS : (h + 1) * ROWS]

    attend(0)
    for copy in w_b:
        copy.wait_recv()
    pairs += [w_pair(3), w_pair(5), w_pair(4)]
    attend(1)
    for copy in pairs:
        copy.wait_recv()

    x_copies = {}

    def product(t, quarter):
        rows = pl.ds(pl.multiple_of(quarter * QUARTER, 16), QUARTER)
        return dot_nn(w_all[rows, :], att[t])

    def project(t):
        for d in (2, 1, 3):
            x_out[t, d - 1] = product(t, x ^ d).astype(jnp.bfloat16)
            x_copies[t, d] = remote(
                x_out.at[t, d - 1], x_in.at[t, d - 1],
                x_send.at[t, d - 1], x_recv.at[t, d - 1], x_peer[d],
            )
        kept[t] = product(t, x)

    slot_side = x % 2

    def last(t, hi, side):
        return pltpu.make_async_remote_copy(
            src_ref=s2_out.at[t], dst_ref=s2_in.at[hi, side],
            send_sem=s2_send.at[t], recv_sem=s2_recv.at[hi, side],
            device_id=targets[t], device_id_type=MESH,
        )

    def deliver(t):
        total = kept[t]
        for d in (1, 3, 2):
            x_copies[t, d].wait_recv()
            total = total + x_in[t, d - 1].astype(jnp.float32)
        s2_out[t] = total.astype(jnp.bfloat16)
        if t:
            last(t, z_hi, slot_side).start()
        else:
            pl.when(jnp.logical_not(home))(lambda: last(t, z_hi, slot_side).start())

            @pl.when(home)
            def _():
                pltpu.make_async_copy(
                    s2_out.at[t], s2_in.at[z_hi, slot_side], s2_recv.at[z_hi, slot_side]
                ).start()

    project(0)
    project(1)
    attend(2)
    project(2)
    deliver(0)
    attend(3)
    project(3)
    deliver(1)
    deliver(2)
    deliver(3)

    for side in range(2):
        for hi in range(2):
            last(1, hi, side).wait_recv()
    both = s2_in[0].astype(jnp.float32) + s2_in[1].astype(jnp.float32)
    both = both.reshape(2 * QUARTER, ROWS)
    out_ref[...] = jnp.transpose(both).astype(jnp.bfloat16)

    for copy in sent:
        copy.wait_send()
    for t in range(1, 4):
        last(t, 0, 0).wait_send()

    @pl.when(jnp.logical_not(home))
    def _():
        last(0, 0, 0).wait_send()


def per_device(queries, key_heads, value_heads, fold_map, partner_map, out_weight):
    vmem = pl.BlockSpec(memory_space=pltpu.VMEM)
    anywhere = pl.BlockSpec(memory_space=pl.ANY)
    smem = pl.BlockSpec(memory_space=pltpu.SMEM)
    bf16, f32 = jnp.bfloat16, jnp.float32
    dma = pltpu.SemaphoreType.DMA
    kv_rows = 2 * ROWS
    return pl.pallas_call(
        kernel,
        out_shape=jax.ShapeDtypeStruct((ROWS, 2 * QUARTER), bf16),
        in_specs=[anywhere, anywhere, anywhere, smem, smem, anywhere],
        out_specs=vmem,
        scratch_shapes=[
            pltpu.VMEM((DEPTH, DIM), bf16),
            pltpu.VMEM((ROWS, DIM), bf16),
            pltpu.VMEM((ROWS, DIM), bf16),
            pltpu.VMEM((DEPTH, DIM), f32),
            pltpu.VMEM((4, DEPTH, DIM), bf16),
            pltpu.VMEM((4, kv_rows, DIM), bf16),
            pltpu.VMEM((N_Y, kv_rows, DIM), bf16),
            pltpu.VMEM((2, 2, kv_rows, DIM), bf16),
            pltpu.VMEM((4, 2, kv_rows, DIM), bf16),
            pltpu.VMEM((16 * CHUNK, DEPTH), bf16),
            pltpu.VMEM((4, DEPTH, ROWS), bf16),
            pltpu.VMEM((4, QUARTER, ROWS), f32),
            pltpu.VMEM((4, 3, QUARTER, ROWS), bf16),
            pltpu.VMEM((4, 3, QUARTER, ROWS), bf16),
            pltpu.VMEM((4, QUARTER, ROWS), bf16),
            pltpu.VMEM((2, 2, QUARTER, ROWS), bf16),
            dma((4,)), dma((8,)), dma((8,)), dma((8,)), dma((8,)), dma((8,)), dma((8,)),
            dma((1,)), dma((1,)), dma((4,)), dma((4,)), dma((4,)), dma((4,)),
            dma((4,)), dma((4,)), dma((4, 3)), dma((4, 3)), dma((4,)), dma((2, 2)),
        ],
        compiler_params=pltpu.CompilerParams(
            collective_id=0, has_side_effects=True, vmem_limit_bytes=56 * 1024 * 1024
        ),
        cost_estimate=pl.CostEstimate(
            flops=1_550_000_000, bytes_accessed=1_000_000, transcendentals=400_000
        ),
    )(
        queries.reshape(ROWS * HEADS, DIM),
        key_heads.reshape(ROWS, DIM),
        value_heads.reshape(ROWS, DIM),
        fold_map,
        partner_map,
        out_weight.T,
    )


def solution(mesh):
    return jax.shard_map(
        per_device,
        mesh=mesh,
        in_specs=(
            P("seq", "head", None),
            P("seq", "head", None),
            P("seq", "head", None),
            P(),
            P(),
            P("head", "seq"),
        ),
        out_specs=P("seq", "head"),
        check_vma=False,
    )
```

time: 86.8 us -> 75.1 us (0.87)
  the two profiles are of different devices: /device:TPU:132 before, /device:TPU:321 now
where the time goes in v2:
time: 75.1 us; the launch traced here: 75 us
  Pallas kernels  73.4 us (98%)
  local copies, waits for them, and re-layouts  1.6 us (2%)
    pallas_call x1, Pallas kernels, per_device(): pl.pallas_call(kernel, out_shape=jax.ShapeDtypeStruct((ROWS, 2 * QUARTER)...  73.4 us
    unnamed x1, local copies, waits for them, and re-layouts  1.6 us

profile of v2, /device:TPU:321, one launch (start us, length us, event | category | flops | bytes accessed | tf_op | source)
XLA Modules:
  0.0 75.0 jit_solution(15486920466146507125)
XLA Ops:
  0.0 73.4 %shard_map.64 = bf16[128,640]{1,0:T(8,128)(2,1)} custom-call(bf16[1024,128]{1,0:T(8,128)(2,1)} %bitcast.4, bf16[128,128]{1,0:T(8,128)(2,1)} %bitcast.6, bf16[128,128]{1,0:T(8,128)(2,1)} %bitcast.7, s32[64]{0:T(128)} %fold_ref.1, s32[2,64]{1,0:T(2,128)} %partner_ref.1, bf16[80,1024]{1,0:T(8,128)(2,1)} %bitcast.5), custom_call_target="tpu_custom_call" | custom-call | flops 1550000000 | bytes 1000000 | tf_op jit(solution)/shard_map/pallas_call | solution.py:297
  73.4 1.6 %copy.8 = bf16[128,640]{1,0:T(8,128)(2,1)} copy(bf16[128,640]{1,0:T(8,128)(2,1)} %shard_map.64) | data formatting | bytes 327680

commit v3 on v2

--- a/solution.py
+++ b/solution.py
@@ -29,7 +29,7 @@
 
 def kernel(
     q_hbm, k_hbm, v_hbm, fold_ref, partner_ref, w_hbm, out_ref,
-    q_in, k_in, v_in, q_wide, q_all, kv_own, kv_y, kv_c, kv_z, w_all, att,
+    q_in, k_in, v_in, q_wide, q_all, kv_own, k_y, v_y, k_c, v_c, kv_z, w_all, att,
     kept, x_out, x_in, s2_out, s2_in,
     in_sem, y_send, y_recv, w_send, w_recv, pair_send, pair_recv, core_send, core_recv,
     q_send, q_recv, own_send, own_recv, z_send, z_recv, x_send, x_recv, s2_send, s2_recv,
@@ -82,8 +82,11 @@
 
     loads[0].wait()
     loads[1].wait()
-    kv_y[0, 0:ROWS, :] = k_in[...]
-    kv_y[0, ROWS:, :] = jnp.transpose(v_in[...].astype(jnp.float32)).astype(jnp.bfloat16)
+    turned = jnp.transpose(v_in[...].astype(jnp.float32)).astype(jnp.bfloat16)
+    kv_own[0, 0:ROWS, :] = k_in[...]
+    kv_own[0, ROWS:, :] = turned
+    k_y[0] = k_in[...]
+    v_y[0] = turned
     loads[2].wait()
     q_wide[...] = q_in[...].astype(jnp.float32)
     for h in range(HEADS):
@@ -104,75 +107,100 @@
         sent.append(copy)
         return copy
 
-    def kv_near(k):
-        return remote(kv_y.at[0], kv_y.at[k], y_send.at[k], y_recv.at[k], y_peer[k])
-
-    def kv_far(i, from_slot, to_slot, peer, part):
+    keys_part, values_part = pl.ds(0, ROWS), pl.ds(ROWS, ROWS)
+    by_y, by_core = (k_y, v_y), (k_c, v_c)
+
+    def kv_copy(kind, i, from_slot, to_slot, peer):
         return remote(
-            kv_y.at[from_slot, part], kv_y.at[to_slot, part],
-            y_send.at[i], y_recv.at[i], y_peer[peer],
-        )
-
-    def w_near(k):
-        return remote(w_all.at[w_own], w_all.at[w_own], w_send.at[k], w_recv.at[k], y_peer[k])
-
-    def w_far(i, slot, peer, first, rows):
-        place = pl.ds(pl.multiple_of(w_rows(slot) + first, 16), rows)
-        return remote(w_all.at[place], w_all.at[place], w_send.at[i], w_recv.at[i], y_peer[peer])
+            by_y[kind].at[from_slot], by_y[kind].at[to_slot],
+            y_send.at[kind, i], y_recv.at[kind, i], y_peer[peer],
+        )
+
+    def w_hop(k):
+        copies = []
+        for way, slot, peer in ((0, k - 1, 1), (1, (9 - k) % 8, 7)):
+            first, rows = (0, CHUNK) if k < 4 else ((0, 48), (48, 32))[way]
+            place = pl.ds(pl.multiple_of(w_rows(slot) + first, 16), rows)
+            sem = (k - 1) * 2 + way
+            copies.append(remote(
+                w_all.at[place], w_all.at[place], w_send.at[sem], w_recv.at[sem], y_peer[peer]
+            ))
+        return copies
 
     def w_pair(k):
         place = pl.ds(w_rows(k), CHUNK)
         return remote(w_all.at[place], w_all.at[place], pair_send.at[k], pair_recv.at[k], other_core)
 
-    kv_a = {k: kv_near(k) for k in (1, 7, 2, 6)}
+    kv_a = {(kind, k): kv_copy(kind, k, 0, k, k) for kind in range(2) for k in (2, 6, 1, 7)}
     q_copy = {
         t: remote(q_all.at[0], q_all.at[t], q_send.at[t], q_recv.at[t], z_peer[t]) for t in (1, 2)
     }
     own_copy = {
-        t: remote(kv_y.at[0], kv_own.at[t], own_send.at[t], own_recv.at[t], z_peer[t])
+        t: remote(kv_own.at[0], kv_own.at[t], own_send.at[t], own_recv.at[t], z_peer[t])
         for t in (1, 2)
     }
-    kv_own[0] = kv_y[0]
     pairs = [w_pair(0)]
-
-    lower, upper, whole = pl.ds(0, ROWS), pl.ds(ROWS, ROWS), pl.ds(0, 2 * ROWS)
-    kv_a[2].wait_recv()
-    kv_b = [kv_far(3, 2, 3, 1, whole), kv_far(4, 2, 4, 2, lower)]
-    kv_a[6].wait_recv()
-    kv_b += [kv_far(5, 6, 5, 7, whole), kv_far(0, 6, 4, 6, upper)]
-    w_a = {k: w_near(k) for k in (1, 7, 2, 6)}
-    kv_a[1].wait_recv()
-    kv_a[7].wait_recv()
-    for copy in kv_b:
-        copy.wait_recv()
 
     partners = [partner_ref[0, seq], partner_ref[1, seq]]
     flips = [partner ^ seq for partner in partners]
-    for i in range(2):
-        kv_c[0, i] = kv_y[(y - (partners[i] >> 1)) & 7]
-    step = remote(kv_c.at[0], kv_c.at[1], core_send.at[0], core_recv.at[0], other_core)
-    step.wait_recv()
-    for i in range(2):
-        kv_z[0, i] = kv_c[flips[i] & 1, i]
-    kv_step = [
-        remote(kv_z.at[0], kv_z.at[t], z_send.at[t], z_recv.at[t], z_peer[t]) for t in (1, 2, 3)
-    ]
+
+    def pass_on(copies):
+        for copy in copies:
+            copy.wait_recv()
+
+    kv_b = [[], []]
+    for kind in range(2):
+        kv_a[kind, 2].wait_recv()
+        kv_b[kind].append(kv_copy(kind, 3, 2, 3, 1))
+        if kind == 0:
+            kv_b[kind].append(kv_copy(kind, 4, 2, 4, 2))
+        kv_a[kind, 6].wait_recv()
+        kv_b[kind].append(kv_copy(kind, 5, 6, 5, 7))
+        if kind == 1:
+            kv_b[kind].append(kv_copy(kind, 4, 6, 4, 6))
+    hop = w_hop(1)
+
+    core_step = []
+    for kind in range(2):
+        pass_on([kv_a[kind, 1], kv_a[kind, 7], *kv_b[kind]])
+        for i in range(2):
+            by_core[kind][0, i] = by_y[kind][(y - (partners[i] >> 1)) & 7]
+        core_step.append(remote(
+            by_core[kind].at[0], by_core[kind].at[1],
+            core_send.at[kind], core_recv.at[kind], other_core,
+        ))
+    z_step = {}
+    for kind in range(2):
+        core_step[kind].wait_recv()
+        for i in range(2):
+            kv_z[0, kind, i] = by_core[kind][flips[i] & 1, i]
+        for t in (1, 2):
+            z_step[t, kind] = remote(
+                kv_z.at[0, kind], kv_z.at[t, kind],
+                z_send.at[t, kind], z_recv.at[t, kind], z_peer[t],
+            )
+
+    pass_on(hop)
+    hop = w_hop(2)
+    pairs += [w_pair(1), w_pair(7)]
+    pass_on(hop)
+    hop = w_hop(3)
+    pairs += [w_pair(2), w_pair(6)]
+    for kind in range(2):
+        z_step[2, kind].wait_recv()
+        z_step[3, kind] = remote(
+            kv_z.at[2, kind], kv_z.at[3, kind], z_send.at[3, kind], z_recv.at[3, kind], z_peer[1]
+        )
+    pass_on(hop)
+    hop = w_hop(4)
+    pairs += [w_pair(3), w_pair(5)]
+    for t in (1, 3):
+        for kind in range(2):
+            z_step[t, kind].wait_recv()
     own_copy[2].wait_recv()
     own_copy[3] = remote(kv_own.at[2], kv_own.at[3], own_send.at[3], own_recv.at[3], z_peer[1])
     q_copy[2].wait_recv()
     q_copy[3] = remote(q_all.at[2], q_all.at[3], q_send.at[3], q_recv.at[3], z_peer[1])
-
-    w_a[2].wait_recv()
-    w_b = [w_far(3, 2, 1, 0, CHUNK), w_far(4, 2, 2, 0, 48)]
-    w_a[6].wait_recv()
-    w_b += [w_far(5, 6, 7, 0, CHUNK), w_far(0, 6, 6, 48, 32)]
-    pairs += [w_pair(2), w_pair(6)]
-    w_a[1].wait_recv()
-    w_a[7].wait_recv()
-    pairs += [w_pair(1), w_pair(7)]
-
-    for copy in kv_step:
-        copy.wait_recv()
 
     def places(fold, offset):
         return offset + jnp.where(
@@ -195,11 +223,13 @@
             hidden.append(jnp.where(seen, 0.0, -jnp.inf).astype(jnp.float32))
         bias = jnp.concatenate(hidden, axis=0)
         bias = jnp.concatenate([bias] * 4, axis=1)
-        blocks = [kv_own[t]]
-        for i in range(2):
-            blocks.append(kv_z[t ^ ((flips[i] >> 4) & 3), i])
-        keys = jnp.concatenate([block[0:ROWS, :] for block in blocks], axis=0)
-        values = jnp.concatenate([block[ROWS:, :] for block in blocks], axis=1)
+        slots = [t ^ ((flip >> 4) & 3) for flip in flips]
+        keys = jnp.concatenate(
+            [kv_own[t, keys_part, :]] + [kv_z[slots[i], 0, i] for i in range(2)], axis=0
+        )
+        values = jnp.concatenate(
+            [kv_own[t, values_part, :]] + [kv_z[slots[i], 1, i] for i in range(2)], axis=1
+        )
         for part in range(2):
             scores = dot_nt(keys, q_all[t, pl.ds(part * 4 * ROWS, 4 * ROWS), :]) * scale + bias
             top = jnp.max(scores, axis=0, keepdims=True)
@@ -211,12 +241,10 @@
                 att[t, pl.ds((part * 4 + h) * DIM, DIM), :] = summed[:, h * ROWS : (h + 1) * ROWS]
 
     attend(0)
-    for copy in w_b:
-        copy.wait_recv()
-    pairs += [w_pair(3), w_pair(5), w_pair(4)]
+    pass_on(hop)
+    pairs.append(w_pair(4))
     attend(1)
-    for copy in pairs:
-        copy.wait_recv()
+    pass_on(pairs)
 
     x_copies = {}
 
@@ -263,9 +291,9 @@
     project(1)
     attend(2)
     project(2)
-    deliver(0)
     attend(3)
     project(3)
+    deliver(0)
     deliver(1)
     deliver(2)
     deliver(3)
@@ -306,9 +334,11 @@
             pltpu.VMEM((DEPTH, DIM), f32),
             pltpu.VMEM((4, DEPTH, DIM), bf16),
             pltpu.VMEM((4, kv_rows, DIM), bf16),
-            pltpu.VMEM((N_Y, kv_rows, DIM), bf16),
-            pltpu.VMEM((2, 2, kv_rows, DIM), bf16),
-            pltpu.VMEM((4, 2, kv_rows, DIM), bf16),
+            pltpu.VMEM((N_Y, ROWS, DIM), bf16),
+            pltpu.VMEM((N_Y, ROWS, DIM), bf16),
+            pltpu.VMEM((2, 2, ROWS, DIM), bf16),
+            pltpu.VMEM((2, 2, ROWS, DIM), bf16),
+            pltpu.VMEM((4, 2, 2, ROWS, DIM), bf16),
             pltpu.VMEM((16 * CHUNK, DEPTH), bf16),
             pltpu.VMEM((4, DEPTH, ROWS), bf16),
             pltpu.VMEM((4, QUARTER, ROWS), f32),
@@ -316,9 +346,9 @@
             pltpu.VMEM((4, 3, QUARTER, ROWS), bf16),
             pltpu.VMEM((4, QUARTER, ROWS), bf16),
             pltpu.VMEM((2, 2, QUARTER, ROWS), bf16),
-            dma((4,)), dma((8,)), dma((8,)), dma((8,)), dma((8,)), dma((8,)), dma((8,)),
-            dma((1,)), dma((1,)), dma((4,)), dma((4,)), dma((4,)), dma((4,)),
-            dma((4,)), dma((4,)), dma((4, 3)), dma((4, 3)), dma((4,)), dma((2, 2)),
+            dma((4,)), dma((2, 8)), dma((2, 8)), dma((8,)), dma((8,)), dma((8,)), dma((8,)),
+            dma((2,)), dma((2,)), dma((4,)), dma((4,)), dma((4,)), dma((4,)),
+            dma((4, 2)), dma((4, 2)), dma((4, 3)), dma((4, 3)), dma((4,)), dma((2, 2)),
         ],
         compiler_params=pltpu.CompilerParams(
             collective_id=0, has_side_effects=True, vmem_limit_bytes=56 * 1024 * 1024

time: 75.1 us -> 72.3 us (0.963)
  the two profiles are of different devices: /device:TPU:321 before, /device:TPU:132 now
where the time goes in v3:
time: 72.3 us; the launch traced here: 72.1 us
  Pallas kernels  70.5 us (98%)
  local copies, waits for them, and re-layouts  1.6 us (2%)
    pallas_call x1, Pallas kernels, per_device(): pl.pallas_call(kernel, out_shape=jax.ShapeDtypeStruct((ROWS, 2 * QUARTER)...  70.5 us
    unnamed x1, local copies, waits for them, and re-layouts  1.6 us

profile of v3, /device:TPU:132, one launch (start us, length us, event | category | flops | bytes accessed | tf_op | source)
XLA Modules:
  0.0 72.1 jit_solution(16433346443660805484)
XLA Ops:
  0.0 70.5 %shard_map.64 = bf16[128,640]{1,0:T(8,128)(2,1)} custom-call(bf16[1024,128]{1,0:T(8,128)(2,1)} %bitcast.4, bf16[128,128]{1,0:T(8,128)(2,1)} %bitcast.6, bf16[128,128]{1,0:T(8,128)(2,1)} %bitcast.7, s32[64]{0:T(128)} %fold_ref.1, s32[2,64]{1,0:T(2,128)} %partner_ref.1, bf16[80,1024]{1,0:T(8,128)(2,1)} %bitcast.5), custom_call_target="tpu_custom_call" | custom-call | flops 1550000000 | bytes 1000000 | tf_op jit(solution)/shard_map/pallas_call | solution.py:325
  70.5 1.6 %copy.8 = bf16[128,640]{1,0:T(8,128)(2,1)} copy(bf16[128,640]{1,0:T(8,128)(2,1)} %shard_map.64) | data formatting | bytes 327680

commit v4 on v3

--- a/solution.py
+++ b/solution.py
@@ -60,7 +60,12 @@
     x_peer = {d: (seq, head ^ d) for d in (1, 2, 3)}
     other_core = (seq ^ 1, head)
 
-    target_head = 2 * z + x // 2
+    def quarter_of(owner):
+        turned = (owner + 2 * (z % 2)) % 4
+        return jnp.where(turned < 2, 2 * turned, 7 - 2 * turned)
+
+    own_quarter = quarter_of(x)
+    target_head = 2 * z + own_quarter // 2
     targets = [(seq ^ (16 * t), target_head) for t in range(4)]
     home = target_head == head
     source_seq = at(head // 2, y, core)
@@ -71,7 +76,8 @@
         pl.semaphore_signal(barrier, inc=1, device_id=peer, device_id_type=MESH)
     for hi in range(2):
         for side in range(2):
-            source_head = hi * 4 + 2 * (head % 2) + side
+            source_x = (head % 2 if side == 0 else 3 - head % 2) + 2 * ((head // 2) % 2)
+            source_head = hi * 4 + source_x % 4
             mine = jnp.logical_and(source_seq == seq, source_head == head)
 
             @pl.when(jnp.logical_not(mine))
@@ -243,7 +249,6 @@
     attend(0)
     pass_on(hop)
     pairs.append(w_pair(4))
-    attend(1)
     pass_on(pairs)
 
     x_copies = {}
@@ -254,14 +259,14 @@
 
     def project(t):
         for d in (2, 1, 3):
-            x_out[t, d - 1] = product(t, x ^ d).astype(jnp.bfloat16)
+            x_out[t, d - 1] = product(t, quarter_of(x ^ d)).astype(jnp.bfloat16)
             x_copies[t, d] = remote(
                 x_out.at[t, d - 1], x_in.at[t, d - 1],
                 x_send.at[t, d - 1], x_recv.at[t, d - 1], x_peer[d],
             )
-        kept[t] = product(t, x)
-
-    slot_side = x % 2
+        kept[t] = product(t, own_quarter)
+
+    slot_side = own_quarter % 2
 
     def last(t, hi, side):
         return pltpu.make_async_remote_copy(
@@ -288,6 +293,7 @@
                 ).start()
 
     project(0)
+    attend(1)
     project(1)
     attend(2)
     project(2)

time: 72.3 us -> 68.9 us (0.953)
  the two profiles are of different devices: /device:TPU:132 before, /device:TPU:158 now
where the time goes in v4:
time: 68.9 us; the launch traced here: 68.5 us
  Pallas kernels  66.9 us (97%)
  local copies, waits for them, and re-layouts  1.6 us (2%)
    pallas_call x1, Pallas kernels, per_device(): pl.pallas_call(kernel, out_shape=jax.ShapeDtypeStruct((ROWS, 2 * QUARTER)...  66.9 us
    unnamed x1, local copies, waits for them, and re-layouts  1.6 us

profile of v4, /device:TPU:158, one launch (start us, length us, event | category | flops | bytes accessed | tf_op | source)
XLA Modules:
  0.0 68.5 jit_solution(1223465059288282326)
XLA Ops:
  0.0 66.9 %shard_map.64 = bf16[128,640]{1,0:T(8,128)(2,1)} custom-call(bf16[1024,128]{1,0:T(8,128)(2,1)} %bitcast.4, bf16[128,128]{1,0:T(8,128)(2,1)} %bitcast.6, bf16[128,128]{1,0:T(8,128)(2,1)} %bitcast.7, s32[64]{0:T(128)} %fold_ref.1, s32[2,64]{1,0:T(2,128)} %partner_ref.1, bf16[80,1024]{1,0:T(8,128)(2,1)} %bitcast.5), custom_call_target="tpu_custom_call" | custom-call | flops 1550000000 | bytes 1000000 | tf_op jit(solution)/shard_map/pallas_call | solution.py:331
  66.9 1.6 %copy.8 = bf16[128,640]{1,0:T(8,128)(2,1)} copy(bf16[128,640]{1,0:T(8,128)(2,1)} %shard_map.64) | data formatting | bytes 327680

commit v5 on v4

--- a/solution.py
+++ b/solution.py
@@ -113,6 +113,10 @@
         sent.append(copy)
         return copy
 
+    def pass_on(copies):
+        for copy in copies:
+            copy.wait_recv()
+
     keys_part, values_part = pl.ds(0, ROWS), pl.ds(ROWS, ROWS)
     by_y, by_core = (k_y, v_y), (k_c, v_c)
 
@@ -122,16 +126,31 @@
             y_send.at[kind, i], y_recv.at[kind, i], y_peer[peer],
         )
 
-    def w_hop(k):
+    w_streams = ((0, 48), (48, CHUNK - 48))
+
+    def w_hop(k, stream):
+        first, rows = w_streams[stream]
         copies = []
         for way, slot, peer in ((0, k - 1, 1), (1, (9 - k) % 8, 7)):
-            first, rows = (0, CHUNK) if k < 4 else ((0, 48), (48, 32))[way]
+            if k == 4 and way != stream:
+                continue
             place = pl.ds(pl.multiple_of(w_rows(slot) + first, 16), rows)
-            sem = (k - 1) * 2 + way
+            sem = (k - 1, way, stream)
             copies.append(remote(
                 w_all.at[place], w_all.at[place], w_send.at[sem], w_recv.at[sem], y_peer[peer]
             ))
         return copies
+
+    hops = {}
+
+    def w_next(k):
+        for stream in range(2):
+            if k > 1:
+                pass_on(hops[k - 1, stream])
+            if k < 5:
+                hops[k, stream] = w_hop(k, stream)
+        for slot in {2: (1, 7), 3: (2, 6), 4: (3, 5), 5: (4,)}.get(k, ()):
+            pairs.append(w_pair(slot))
 
     def w_pair(k):
         place = pl.ds(w_rows(k), CHUNK)
@@ -149,10 +168,6 @@
 
     partners = [partner_ref[0, seq], partner_ref[1, seq]]
     flips = [partner ^ seq for partner in partners]
-
-    def pass_on(copies):
-        for copy in copies:
-            copy.wait_recv()
 
     kv_b = [[], []]
     for kind in range(2):
@@ -164,7 +179,7 @@
         kv_b[kind].append(kv_copy(kind, 5, 6, 5, 7))
         if kind == 1:
             kv_b[kind].append(kv_copy(kind, 4, 6, 4, 6))
-    hop = w_hop(1)
+    w_next(1)
 
     core_step = []
     for kind in range(2):
@@ -186,27 +201,21 @@
                 z_send.at[t, kind], z_recv.at[t, kind], z_peer[t],
             )
 
-    pass_on(hop)
-    hop = w_hop(2)
-    pairs += [w_pair(1), w_pair(7)]
-    pass_on(hop)
-    hop = w_hop(3)
-    pairs += [w_pair(2), w_pair(6)]
+    w_next(2)
+    w_next(3)
     for kind in range(2):
         z_step[2, kind].wait_recv()
         z_step[3, kind] = remote(
             kv_z.at[2, kind], kv_z.at[3, kind], z_send.at[3, kind], z_recv.at[3, kind], z_peer[1]
         )
-    pass_on(hop)
-    hop = w_hop(4)
-    pairs += [w_pair(3), w_pair(5)]
-    for t in (1, 3):
-        for kind in range(2):
-            z_step[t, kind].wait_recv()
     own_copy[2].wait_recv()
     own_copy[3] = remote(kv_own.at[2], kv_own.at[3], own_send.at[3], own_recv.at[3], z_peer[1])
     q_copy[2].wait_recv()
     q_copy[3] = remote(q_all.at[2], q_all.at[3], q_send.at[3], q_recv.at[3], z_peer[1])
+    w_next(4)
+    for t in (1, 3):
+        for kind in range(2):
+            z_step[t, kind].wait_recv()
 
     def places(fold, offset):
         return offset + jnp.where(
@@ -247,8 +256,7 @@
                 att[t, pl.ds((part * 4 + h) * DIM, DIM), :] = summed[:, h * ROWS : (h + 1) * ROWS]
 
     attend(0)
-    pass_on(hop)
-    pairs.append(w_pair(4))
+    w_next(5)
     pass_on(pairs)
 
     x_copies = {}
@@ -352,7 +360,7 @@
             pltpu.VMEM((4, 3, QUARTER, ROWS), bf16),
             pltpu.VMEM((4, QUARTER, ROWS), bf16),
             pltpu.VMEM((2, 2, QUARTER, ROWS), bf16),
-            dma((4,)), dma((2, 8)), dma((2, 8)), dma((8,)), dma((8,)), dma((8,)), dma((8,)),
+            dma((4,)), dma((2, 8)), dma((2, 8)), dma((4, 2, 2)), dma((4, 2, 2)), dma((8,)), dma((8,)),
             dma((2,)), dma((2,)), dma((4,)), dma((4,)), dma((4,)), dma((4,)),
             dma((4, 2)), dma((4, 2)), dma((4, 3)), dma((4, 3)), dma((4,)), dma((2, 2)),
         ],

time: 68.9 us -> 68.6 us (level)
  no operation moved by 1% of the time
where the time goes in v5:
time: 68.6 us; the launch traced here: 68.4 us
  Pallas kernels  66.8 us (97%)
  local copies, waits for them, and re-layouts  1.6 us (2%)
    pallas_call x1, Pallas kernels, per_device(): pl.pallas_call(kernel, out_shape=jax.ShapeDtypeStruct((ROWS, 2 * QUARTER)...  66.8 us
    unnamed x1, local copies, waits for them, and re-layouts  1.6 us

profile of v5, /device:TPU:158, one launch (start us, length us, event | category | flops | bytes accessed | tf_op | source)
XLA Modules:
  0.0 68.4 jit_solution(12016431604366639843)
XLA Ops:
  0.0 66.8 %shard_map.64 = bf16[128,640]{1,0:T(8,128)(2,1)} custom-call(bf16[1024,128]{1,0:T(8,128)(2,1)} %bitcast.4, bf16[128,128]{1,0:T(8,128)(2,1)} %bitcast.6, bf16[128,128]{1,0:T(8,128)(2,1)} %bitcast.7, s32[64]{0:T(128)} %fold_ref.1, s32[2,64]{1,0:T(2,128)} %partner_ref.1, bf16[80,1024]{1,0:T(8,128)(2,1)} %bitcast.5), custom_call_target="tpu_custom_call" | custom-call | flops 1550000000 | bytes 1000000 | tf_op jit(solution)/shard_map/pallas_call | solution.py:339
  66.8 1.6 %copy.8 = bf16[128,640]{1,0:T(8,128)(2,1)} copy(bf16[128,640]{1,0:T(8,128)(2,1)} %shard_map.64) | data formatting | bytes 327680

commit v6 on v5

--- a/solution.py
+++ b/solution.py
@@ -28,9 +28,9 @@
 
 
 def kernel(
-    q_hbm, k_hbm, v_hbm, fold_ref, partner_ref, w_hbm, out_ref,
+    q_hbm, k_hbm, v_hbm, fold_ref, partner_ref, w_hbm, s2_in,
     q_in, k_in, v_in, q_wide, q_all, kv_own, k_y, v_y, k_c, v_c, kv_z, w_all, att,
-    kept, x_out, x_in, s2_out, s2_in,
+    kept, x_out, x_in, s2_out,
     in_sem, y_send, y_recv, w_send, w_recv, pair_send, pair_recv, core_send, core_recv,
     q_send, q_recv, own_send, own_recv, z_send, z_recv, x_send, x_recv, s2_send, s2_recv,
 ):
@@ -315,10 +315,6 @@
     for side in range(2):
         for hi in range(2):
             last(1, hi, side).wait_recv()
-    both = s2_in[0].astype(jnp.float32) + s2_in[1].astype(jnp.float32)
-    both = both.reshape(2 * QUARTER, ROWS)
-    out_ref[...] = jnp.transpose(both).astype(jnp.bfloat16)
-
     for copy in sent:
         copy.wait_send()
     for t in range(1, 4):
@@ -330,17 +326,16 @@
 
 
 def per_device(queries, key_heads, value_heads, fold_map, partner_map, out_weight):
-    vmem = pl.BlockSpec(memory_space=pltpu.VMEM)
     anywhere = pl.BlockSpec(memory_space=pl.ANY)
     smem = pl.BlockSpec(memory_space=pltpu.SMEM)
     bf16, f32 = jnp.bfloat16, jnp.float32
     dma = pltpu.SemaphoreType.DMA
     kv_rows = 2 * ROWS
-    return pl.pallas_call(
+    halves = pl.pallas_call(
         kernel,
-        out_shape=jax.ShapeDtypeStruct((ROWS, 2 * QUARTER), bf16),
+        out_shape=jax.ShapeDtypeStruct((2, 2, QUARTER, ROWS), bf16),
         in_specs=[anywhere, anywhere, anywhere, smem, smem, anywhere],
-        out_specs=vmem,
+        out_specs=anywhere,
         scratch_shapes=[
             pltpu.VMEM((DEPTH, DIM), bf16),
             pltpu.VMEM((ROWS, DIM), bf16),
@@ -359,7 +354,6 @@
             pltpu.VMEM((4, 3, QUARTER, ROWS), bf16),
             pltpu.VMEM((4, 3, QUARTER, ROWS), bf16),
             pltpu.VMEM((4, QUARTER, ROWS), bf16),
-            pltpu.VMEM((2, 2, QUARTER, ROWS), bf16),
             dma((4,)), dma((2, 8)), dma((2, 8)), dma((4, 2, 2)), dma((4, 2, 2)), dma((8,)), dma((8,)),
             dma((2,)), dma((2,)), dma((4,)), dma((4,)), dma((4,)), dma((4,)),
             dma((4, 2)), dma((4, 2)), dma((4, 3)), dma((4, 3)), dma((4,)), dma((2, 2)),
@@ -377,7 +371,8 @@
         fold_map,
         partner_map,
         out_weight.T,
-    )
+    ).astype(f32)
+    return (halves[0] + halves[1]).reshape(2 * QUARTER, ROWS).T.astype(bf16)
 
 
 def solution(mesh):

time: 68.6 us -> 68.2 us (level)
  other arithmetic: 0 us -> 1.05 us
  local copies, waits for them, and re-layouts: 1.6 us -> 0.81 us
  Pallas kernels: 66.8 us -> 66.1 us
    unnamed x1 -> x0, local copies, waits for them, and re-layouts: 1.6 us -> none
    convert_element_type x0 -> x2, other arithmetic: none -> 1.05 us  [the longest x1 1.02 us: per_device(): halves = pl.pallas_call(kernel, out_shape=jax.ShapeDtypeStruct((2, 2, QUA...]
    convert_element_type x0 -> x1, local copies, waits for them, and re-layouts: none -> 0.81 us  [per_device(): return (halves[0] + halves[1]).reshape(2 * QUARTER, ROWS).T.astype(bf16)]
    pallas_call x1, Pallas kernels: 66.8 us -> 66.1 us  [per_device(): pl.pallas_call(kernel, out_shape=jax.ShapeDtypeStruct((2, 2, QUARTER, ROW...]
where the time goes in v6:
time: 68.2 us; the launch traced here: 68 us
  Pallas kernels  66.1 us (97%)
  other arithmetic  1.05 us (2%)
  local copies, waits for them, and re-layouts  0.81 us (1%)
    pallas_call x1, Pallas kernels, per_device(): pl.pallas_call(kernel, out_shape=jax.ShapeDtypeStruct((2, 2, QUARTER, ROW...  66.1 us

profile of v6, /device:TPU:158, one launch (start us, length us, event | category | flops | bytes accessed | tf_op | source)
XLA Modules:
  0.0 68.0 jit_solution(2231507229811960231)
XLA Ops:
  0.0 66.1 %shard_map.64 = bf16[2,2,320,128]{3,2,1,0:T(8,128)(2,1)} custom-call(bf16[1024,128]{1,0:T(8,128)(2,1)} %bitcast.7, bf16[128,128]{1,0:T(8,128)(2,1)} %bitcast.9, bf16[128,128]{1,0:T(8,128)(2,1)} %bitcast.10, s32[64]{0:T(128)} %fold_ref.1, s32[2,64]{1,0:T(2,128)} %partner_ref.1, bf16[80,1024]{1,0:T(8,128)(2,1)} %bitcast.8), custom_call_target="tpu_custom_call" | custom-call | flops 1550000000 | bytes 1000000 | tf_op jit(solution)/shard_map/pallas_call | solution.py:334
  66.1 1.0 %convert_element_type.12 = f32[2,2,320,128]{3,2,1,0:T(8,128)S(1)} convert(bf16[2,2,320,128]{3,2,1,0:T(8,128)(2,1)} %shard_map.64) | non-fusion elementwise | flops 163840 | bytes 983040 | tf_op jit(solution)/shard_map/convert_element_type | solution.py:374
  67.2 0.8 %copy.7 = bf16[640,128]{0,1:T(8,128)(2,1)} copy(bf16[640,128]{1,0:T(8,128)(2,1)S(1)} %bitcast.6) | data formatting | bytes 327680 | tf_op jit(solution)/shard_map/convert_element_type | solution.py:375
  (1 shorter events, 0.0 us)

commit v7 on v6

--- a/solution.py
+++ b/solution.py
@@ -132,13 +132,18 @@
         first, rows = w_streams[stream]
         copies = []
         for way, slot, peer in ((0, k - 1, 1), (1, (9 - k) % 8, 7)):
-            if k == 4 and way != stream:
-                continue
             place = pl.ds(pl.multiple_of(w_rows(slot) + first, 16), rows)
             sem = (k - 1, way, stream)
             copies.append(remote(
                 w_all.at[place], w_all.at[place], w_send.at[sem], w_recv.at[sem], y_peer[peer]
             ))
+        if k == 3:
+            slot = (2, 6)[stream]
+            place = pl.ds(pl.multiple_of(w_rows(slot) + first, 16), rows)
+            sem = (3, stream, 0)
+            copies.append(remote(
+                w_all.at[place], w_all.at[place], w_send.at[sem], w_recv.at[sem], y_peer[slot]
+            ))
         return copies
 
     hops = {}
@@ -147,9 +152,9 @@
         for stream in range(2):
             if k > 1:
                 pass_on(hops[k - 1, stream])
-            if k < 5:
+            if k < 4:
                 hops[k, stream] = w_hop(k, stream)
-        for slot in {2: (1, 7), 3: (2, 6), 4: (3, 5), 5: (4,)}.get(k, ()):
+        for slot in {2: (1, 7), 3: (2, 6), 4: (3, 5, 4)}.get(k, ()):
             pairs.append(w_pair(slot))
 
     def w_pair(k):
@@ -256,7 +261,6 @@
                 att[t, pl.ds((part * 4 + h) * DIM, DIM), :] = summed[:, h * ROWS : (h + 1) * ROWS]
 
     attend(0)
-    w_next(5)
     pass_on(pairs)
 
     x_copies = {}

time: 68.2 us -> 67.6 us (level)
  the two profiles are of different devices: /device:TPU:158 before, /device:TPU:128 now
where the time goes in v7:
time: 67.6 us; the launch traced here: 67.4 us
  Pallas kernels  65.6 us (97%)
  other arithmetic  1.05 us (2%)
  local copies, waits for them, and re-layouts  0.81 us (1%)
    pallas_call x1, Pallas kernels, per_device(): pl.pallas_call(kernel, out_shape=jax.ShapeDtypeStruct((2, 2, QUARTER, ROW...  65.6 us

profile of v7, /device:TPU:128, one launch (start us, length us, event | category | flops | bytes accessed | tf_op | source)
XLA Modules:
  0.0 67.4 jit_solution(5440168686858613167)
XLA Ops:
  0.0 65.6 %shard_map.64 = bf16[2,2,320,128]{3,2,1,0:T(8,128)(2,1)} custom-call(bf16[1024,128]{1,0:T(8,128)(2,1)} %bitcast.7, bf16[128,128]{1,0:T(8,128)(2,1)} %bitcast.9, bf16[128,128]{1,0:T(8,128)(2,1)} %bitcast.10, s32[64]{0:T(128)} %fold_ref.1, s32[2,64]{1,0:T(2,128)} %partner_ref.1, bf16[80,1024]{1,0:T(8,128)(2,1)} %bitcast.8), custom_call_target="tpu_custom_call" | custom-call | flops 1550000000 | bytes 1000000 | tf_op jit(solution)/shard_map/pallas_call | solution.py:338
  65.6 1.0 %convert_element_type.12 = f32[2,2,320,128]{3,2,1,0:T(8,128)S(1)} convert(bf16[2,2,320,128]{3,2,1,0:T(8,128)(2,1)} %shard_map.64) | non-fusion elementwise | flops 163840 | bytes 983040 | tf_op jit(solution)/shard_map/convert_element_type | solution.py:378
  66.6 0.8 %copy.7 = bf16[640,128]{0,1:T(8,128)(2,1)} copy(bf16[640,128]{1,0:T(8,128)(2,1)S(1)} %bitcast.6) | data formatting | bytes 327680 | tf_op jit(solution)/shard_map/convert_element_type | solution.py:379
  (1 shorter events, 0.0 us)
